TPU v7x, 32 devices: a whole 2x2x4 slice. The times are simulated.
32 devices in a mesh: tiles: 4 (over z), rows: 8 (over y, x, core).
Axes of the slice: x: 2, y: 2, z: 4, core: 2. Of those that a mesh axis runs over, the one named last changes fastest.
Arguments:
- tile_values: bfloat16 [32, 8, 1024, 1024], P(('tiles', 'rows')), may hold values from -6 to 6
- tile_coords: int32 [32, 8, 4], P(('tiles', 'rows')), may hold values from 0 to 95, as said below
- tile_count: int32 [32], P(('tiles', 'rows')), may hold values from 4 to 8, as said below
- factors: float32 [4, 3072, 256], P(None, 'rows'), may hold values from -3 to 3
Outputs:
- updated: float32 [4, 3072, 256], P(None, 'rows')
Inputs may be any that keep to these rules, and one draw needn't show every extreme that they name: `tile_coords`: over the live slots of one device, the four modes together name blocks of one row owner (block index // 12) at most 4 times; on every device some owner is named exactly 4 times. The same block may appear in several tiles. Slot 0 is always live. Slots from tile_count[d] on are ignored; some device has all slots live.
All inputs are finite; a program needn't handle non-finite values.
Results may differ from a plain program's by a relative error of at most 0.0033.
Values may be sent and summed in bfloat16 or wider, within the bound.
A program may use at most 128 MiB of HBM per device.

v0:
```python
import jax
import jax.numpy as jnp
from jax import lax
from jax.sharding import PartitionSpec as P

TILE = 32


step_size = 0.02


def tile_grads(tile_block, blocks):
    widened = blocks.astype(jnp.float32)
    mode_one, mode_two, mode_three, mode_four = (widened[0], widened[1], widened[2], widened[3])
    tile_edge = mode_one.shape[0]
    pair_ab = (
        (mode_one[:, None, :] * mode_two[None, :, :])
        .reshape(tile_edge * tile_edge, -1)
        .astype(jnp.bfloat16)
    )
    pair_cd = (
        (mode_three[:, None, :] * mode_four[None, :, :])
        .reshape(tile_edge * tile_edge, -1)
        .astype(jnp.bfloat16)
    )
    model_values = lax.dot_general(
        pair_ab, pair_cd, (((1,), (1,)), ((), ())), preferred_element_type=jnp.float32
    )
    misfit = jnp.clip(model_values - tile_block.astype(jnp.float32), -1.0, 1.0).astype(jnp.bfloat16)
    left_terms = jnp.dot(misfit, pair_cd, preferred_element_type=jnp.float32).reshape(
        tile_edge, tile_edge, -1
    )
    right_terms = lax.dot_general(
        misfit, pair_ab, (((0,), (0,)), ((), ())), preferred_element_type=jnp.float32
    ).reshape(tile_edge, tile_edge, -1)
    grad_one = jnp.sum(left_terms * mode_two[None, :, :], axis=1)
    grad_two = jnp.sum(left_terms * mode_one[:, None, :], axis=0)
    grad_three = jnp.sum(right_terms * mode_four[None, :, :], axis=1)
    grad_four = jnp.sum(right_terms * mode_three[:, None, :], axis=0)
    return jnp.stack([grad_one, grad_two, grad_three, grad_four])


def on_device(tile_values, tile_coords, tile_count, factors):
    tile_stack = tile_values[0]
    coords = tile_coords[0]
    live_count = tile_count[0]
    slot_total = coords.shape[0]
    row_peers = lax.axis_size("rows")
    local_blocks = factors.shape[1] // TILE
    narrow = factors.astype(jnp.bfloat16)
    row_index = coords[:, :, None] * TILE + jnp.arange(TILE)[None, None, :]
    mode_index = jnp.arange(4)[None, :, None]
    everything = lax.all_gather(narrow, "rows", axis=1, tiled=True)
    blocks = everything[mode_index, row_index]

    def accumulate(slot_idx, running):
        gradient = tile_grads(tile_stack[slot_idx], blocks[slot_idx])
        return lax.dynamic_update_index_in_dim(running, gradient, slot_idx, 0)

    grad_blocks = lax.fori_loop(
        0, live_count, accumulate, jnp.zeros((slot_total, 4, TILE, factors.shape[2]), jnp.float32)
    )
    dense_grads = jnp.zeros((4, row_peers * local_blocks * TILE, factors.shape[2]), jnp.float32)
    dense_grads = dense_grads.at[mode_index, row_index].add(grad_blocks)
    partial_sum = lax.psum_scatter(dense_grads, "rows", scatter_dimension=1, tiled=True)
    total_grad = lax.psum(partial_sum, "tiles")
    return factors - step_size * total_grad


def solution(mesh):
    return jax.shard_map(
        on_device,
        mesh=mesh,
        in_specs=(
            P(("tiles", "rows"), None, None, None),
            P(("tiles", "rows"), None, None),
            P(("tiles", "rows")),
            P(None, "rows", None),
        ),
        out_specs=P(None, "rows", None),
        check_vma=False,
    )
```

profile of v0, /device:TPU:0, one launch (start us, length us, event | category | flops | bytes accessed | tf_op | source)
XLA Modules:
  0.0 334.0 jit_solution(17724332897151669849)
XLA Ops:
  6.5 2.4 convert_element_type.48
  8.9 0.0 all-gather.2.cloned.1.call-update
  8.9 0.0 reduce-scatter.2.cloned.1.call-start
  9.0 0.1 copy.8
  9.1 0.1 shift-left_or_fusion
  9.2 0.1 reshape.83
  9.3 0.1 multiply_reduce_fusion.4
  9.4 0.1 and_reduce_fusion
  9.5 0.1 reshape.89
  9.6 47.9 %all-gather.2.cloned.1.call-done = bf16[4,3072,256]{2,1,0:T(8,128)(2,1)} async-done(((bf16[4,384,256]{2,1,0:T(8,128)(2,1)}), bf16[4,3072,256]{2,1,0:T(8,128)(2,1)}) %all-gather.2.cloned.1.call-update) | async-done | bytes 6291472 | tf_op jit(solution)/shard_map/all_gather | solution.py:53
  57.5 13.2 %gather_fusion = bf16[1024,256]{1,0:T(8,128)(2,1)S(1)} fusion(bf16[4,3072,256]{2,1,0:T(8,128)(2,1)} %all-gather.2.cloned.1.call-done, s32[1024]{0:T(1024)S(1)} %reshape.83), kind=kCustom, calls=%fused_computation | custom fusion | bytes 1056768 | tf_op jit(solution)/shard_map/gather | solution.py:54
  70.7 1.1 broadcast_in_dim.12
  71.8 49.0 %while.10 = (s32[]{:T(128)}, f32[8,4,32,256]{3,2,1,0:T(8,128)}, s32[]{:T(128)}, bf16[8,4,32,256]{3,2,1,0:T(8,128)(2,1)S(1)}, bf16[8,1024,1024]{2,1,0:T(8,128)(2,1)}, /*index=5*/s32[]{:T(128)}, s32[]{:T(128)}, s32[]{:T(128)}) while((s32[]{:T(128)}, f32[8,4,32,256]{3,2,1,0:T(8,128)}, s32[]{:T(128)}, bf16[8,4,32,256]{3,2,1,0:T(8,128)(2,1)S(1)}, ...), condition=%wide.region_5.6_spmd, body=%wide.region_0.5_spmd.sunk | while | flops 1618051072 | bytes 16842892 | solution.py:60
  72.5 0.3 multiply_convert_fusion.3
  72.8 2.3 fusion.25
  75.2 0.7 multiply_reduce_fusion.8
  75.9 2.6 copy.10
  78.5 2.3 multiply_reduce_fusion.7
  80.8 0.7 fusion.26
  82.2 0.3 multiply_convert_fusion.3
  82.5 2.3 fusion.25
  84.8 0.7 multiply_reduce_fusion.8
  85.6 2.6 copy.10
  88.1 2.3 multiply_reduce_fusion.7
  90.4 0.7 fusion.26
  91.8 0.3 multiply_convert_fusion.3
  92.1 2.3 fusion.25
  94.5 0.7 multiply_reduce_fusion.8
  95.2 2.6 copy.10
  97.8 2.3 multiply_reduce_fusion.7
  100.1 0.7 fusion.26
  101.5 0.3 multiply_convert_fusion.3
  101.8 2.3 fusion.25
  104.1 0.7 multiply_reduce_fusion.8
  104.9 2.6 copy.10
  107.5 2.3 multiply_reduce_fusion.7
  109.8 0.7 fusion.26
  111.2 0.3 multiply_convert_fusion.3
  111.5 2.3 fusion.25
  113.8 0.7 multiply_reduce_fusion.8
  114.5 2.6 copy.10
  117.1 2.3 multiply_reduce_fusion.7
  119.4 0.7 fusion.26
  120.8 11.9 %scatter_custom_fusion = f32[12288,256]{1,0:T(8,128)} fusion(s32[1024]{0:T(1024)S(1)} %reshape.89, f32[1024,256]{1,0:T(8,128)} %bitcast.93, f32[]{:T(128)} %constant.3.clone.1), kind=kCustom, calls=%fused_computation.18 | custom fusion | flops 262144 | bytes 12583424
  132.7 0.0 all-reduce.2.cloned.1.call-start
  132.7 120.5 %reduce-scatter.2.cloned.1.call-done = f32[4,384,256]{2,1,0:T(8,128)} async-done(((f32[4,3072,256]{2,1,0:T(8,128)}), f32[4,384,256]{2,1,0:T(8,128)}) %reduce-scatter.2.cloned.1.call-update) | async-done | bytes 1572880 | tf_op jit(solution)/shard_map/reduce_scatter | solution.py:65
  253.2 71.5 %all-reduce.2.cloned.1.call-done = f32[4,384,256]{2,1,0:T(8,128)} async-done(((f32[4,384,256]{2,1,0:T(8,128)}), f32[4,384,256]{2,1,0:T(8,128)}) %all-reduce.2.cloned.1.call-update) | async-done | bytes 1572880 | tf_op jit(solution)/shard_map/psum | solution.py:66
  324.8 2.8 multiply_subtract_fusion
  (24 shorter events, 0.2 us)
Async XLA Ops:
  6.5 2.7 copy-start.3
  6.5 2.8 copy-start.2
  6.5 2.5 copy-start.1
  6.5 51.0 %all-gather.2.cloned.1.call-start = ((), (), s32[]{:S(2)}) async-start(), calls=%async_computation.1 | async-start | bytes 7077888 | tf_op jit(solution)/shard_map/all_gather | solution.py:53
  8.9 244.3 %reduce-scatter.2.cloned.1.call-start = ((), (), s32[]{:S(2)}) async-start(), calls=%async_computation.2 | async-start | bytes 14155776 | tf_op jit(solution)/shard_map/reduce_scatter | solution.py:65
  132.7 192.1 %copy-start = (f32[4,384,256]{2,1,0:T(8,128)S(1)}, f32[4,384,256]{2,1,0:T(8,128)}, u32[]{:S(2)}) copy-start(f32[4,384,256]{2,1,0:T(8,128)} %param.9) | copy-start | bytes 4718596
  132.7 192.1 %all-reduce.2.cloned.1.call-start = ((), (), s32[]{:S(2)}) async-start(), calls=%async_computation.3 | async-start | bytes 3145728 | tf_op jit(solution)/shard_map/psum | solution.py:66
Sparse Core Ops, SparseCore 0:
  9.3 48.2 all-gather.1
  132.8 120.3 reduce-scatter.1
  255.6 69.1 all-reduce.1
where the time goes:
time: 335 us; the launch traced here: 334 us
  waiting for transfers between devices  240 us (72%)
  local copies, waits for them, and re-layouts  27.5 us (8%)
  matrix products  26.9 us (8%)
  other arithmetic  22.2 us (7%)
  between operations  13.2 us (4%)
  loops' own time  4.18 us (1%)
    reduce_scatter x1, waiting for transfers between devices, on_device(): lax.psum_scatter(dense_grads, 'rows', scatter_dimension=1, tiled=True)  120 us
    psum x1, waiting for transfers between devices, on_device(): total_grad = lax.psum(partial_sum, 'tiles')  71.5 us
    all_gather x1, waiting for transfers between devices, on_device(): everything = lax.all_gather(narrow, 'rows', axis=1, tiled=True)  47.9 us
    gather x1, local copies, waits for them, and re-layouts, on_device(): blocks = everything[mode_index, row_index]  13.2 us
    dot_general x5, local copies, waits for them, and re-layouts, tile_grads(): lax.dot_general(misfit, pair_ab, (((0,), (0,)), ((), ())), preferred_elem...  12.9 us
    unnamed x4, other arithmetic  12.1 us
    dot_general x5, matrix products, tile_grads(): lax.dot_general(pair_ab, pair_cd, (((1,), (1,)), ((), ())), preferred_ele...  11.7 us
    dot_general x5, matrix products, tile_grads(): lax.dot_general(misfit, pair_ab, (((0,), (0,)), ((), ())), preferred_elem...  11.6 us
  transfers between devices with their start and end apart: 3, of which 3 were waited for; matrix products, arithmetic and copies ran while one was open for 0% of the time, Pallas kernels for 0%

commit v1 on v0

v1 whole, which is shorter than its diff:
```python
import functools

import jax
import jax.numpy as jnp
from jax import lax
from jax.experimental import pallas as pl
from jax.experimental.pallas import tpu as pltpu
from jax.sharding import PartitionSpec as P

TILE = 32
CAP = 4
LANES = 128
MESH = pl.DeviceIdType.MESH

step_size = 0.02


def position(peers, rows):
    return lax.axis_index("tiles") * rows + lax.axis_index("rows")


def place(index, rows):
    return {"tiles": index // rows, "rows": lax.rem(index, rows)}


def enter(me, peers, rows):
    barrier = pltpu.get_barrier_semaphore()

    @pl.loop(1, peers)
    def _(k):
        other = lax.rem(me + k, peers)
        pl.semaphore_signal(barrier, inc=1, device_id=place(other, rows), device_id_type=MESH)

    pl.semaphore_wait(barrier, peers - 1)


def fetch_kernel(tiles, rows, want_ref, factors_ref, names_ref, blocks_ref, packed, scalars, name_send, name_recv, block_send, block_recv, local_sem):
    peers = tiles * rows
    my_tile, my_row = lax.axis_index("tiles"), lax.axis_index("rows")
    me = my_tile * rows + my_row
    enter(me, peers, rows)
    names_ref[me] = want_ref[...]

    def name_copy(other, slot, sem):
        return pltpu.make_async_remote_copy(
            src_ref=want_ref, dst_ref=names_ref.at[slot], send_sem=name_send.at[sem], recv_sem=name_recv.at[slot],
            device_id=place(other, rows), device_id_type=MESH)

    @pl.loop(1, rows)
    def _(k):
        other = my_tile * rows + lax.rem(my_row + k, rows)
        name_copy(other, me, other).start()

    @pl.loop(1, tiles)
    def _(j):
        @pl.loop(0, rows)
        def _(k):
            other = lax.rem(my_tile + j, tiles) * rows + lax.rem(my_row + k, rows)
            name_copy(other, me, other).start()

    @pl.loop(1, rows)
    def _(k):
        other = my_tile * rows + lax.rem(my_row + k, rows)
        name_copy(other, other, other).wait_recv()

    bring = pltpu.make_async_copy(names_ref.at[pl.ds(my_tile * rows, rows)], scalars, local_sem)
    bring.start()
    bring.wait()

    def block_copy(peer, slot):
        return pltpu.make_async_remote_copy(
            src_ref=packed.at[peer], dst_ref=blocks_ref.at[slot], send_sem=block_send.at[peer], recv_sem=block_recv.at[slot],
            device_id=place(my_tile * rows + peer, rows), device_id_type=MESH)

    def read(peer, rank):
        return factors_ref[jnp.maximum(scalars[peer, 0, my_row * CAP + rank], 0)].astype(jnp.bfloat16)

    @pl.loop(1, rows)
    def _(k):
        peer = lax.rem(my_row + k, rows)
        for rank in range(CAP):
            packed[peer, pl.ds(rank * TILE, TILE), :] = read(peer, rank)
        block_copy(peer, my_row).start()

    for rank in range(CAP):
        blocks_ref[my_row, pl.ds(rank * TILE, TILE), :] = read(my_row, rank)

    @pl.loop(1, rows)
    def _(k):
        peer = lax.rem(my_row + k, rows)
        block_copy(peer, peer).wait_recv()
        block_copy(peer, my_row).wait_send()
        other = my_tile * rows + peer
        name_copy(other, me, other).wait_send()

    @pl.loop(1, tiles)
    def _(j):
        @pl.loop(0, rows)
        def _(k):
            other = lax.rem(my_tile + j, tiles) * rows + lax.rem(my_row + k, rows)
            name_copy(other, other, other).wait_recv()
            name_copy(other, me, other).wait_send()


def fetch(want, factors, tiles, rows):
    rank = factors.shape[2]
    peers = tiles * rows
    return pl.pallas_call(
        functools.partial(fetch_kernel, tiles, rows),
        out_shape=(
            jax.ShapeDtypeStruct((peers, 1, LANES), jnp.int32),
            jax.ShapeDtypeStruct((rows, CAP * TILE, rank), jnp.bfloat16),
        ),
        in_specs=[pl.BlockSpec(memory_space=pltpu.VMEM)] * 2,
        out_specs=[pl.BlockSpec(memory_space=pltpu.VMEM)] * 2,
        scratch_shapes=[
            pltpu.VMEM((rows, CAP * TILE, rank), jnp.bfloat16),
            pltpu.SMEM((rows, 1, LANES), jnp.int32),
            pltpu.SemaphoreType.DMA((peers,)),
            pltpu.SemaphoreType.DMA((peers,)),
            pltpu.SemaphoreType.DMA((rows,)),
            pltpu.SemaphoreType.DMA((rows,)),
            pltpu.SemaphoreType.DMA,
        ],
        compiler_params=pltpu.CompilerParams(collective_id=0, has_side_effects=True, vmem_limit_bytes=32 << 20),
        name="fetch_blocks",
    )(want, factors)


def tile_kernel(pos_ref, count_ref, tile_ref, blocks_ref, grads_ref, pair_ab, pair_cd, misfit):
    slot = pl.program_id(0)
    edge = TILE
    chunk = 256
    group = chunk // edge
    rank = blocks_ref.shape[2]

    @pl.when(slot < count_ref[0])
    def _():
        one, two, three, four = (blocks_ref[pos_ref[slot * 4 + mode]].astype(jnp.float32) for mode in range(4))
        for part in range(edge // group):
            lines = slice(part * group, (part + 1) * group)
            place_at = pl.ds(part * chunk, chunk)
            pair_ab[place_at, :] = (one[lines][:, None, :] * two[None, :, :]).reshape(chunk, rank).astype(jnp.bfloat16)
            pair_cd[place_at, :] = (three[lines][:, None, :] * four[None, :, :]).reshape(chunk, rank).astype(jnp.bfloat16)
        second = jnp.zeros((edge, rank), jnp.float32)
        for part in range(edge // group):
            lines = slice(part * group, (part + 1) * group)
            place_at = pl.ds(part * chunk, chunk)
            model = lax.dot_general(pair_ab[place_at, :], pair_cd[...], (((1,), (1,)), ((), ())), preferred_element_type=jnp.float32)
            off = jnp.clip(model - tile_ref[0, place_at, :].astype(jnp.float32), -1.0, 1.0).astype(jnp.bfloat16)
            misfit[place_at, :] = off
            left = jnp.dot(off, pair_cd[...], preferred_element_type=jnp.float32).reshape(group, edge, rank)
            grads_ref[0, 0, lines, :] = jnp.sum(left * two[None, :, :], axis=1)
            second = second + jnp.sum(left * one[lines][:, None, :], axis=0)
        grads_ref[0, 1] = second
        fourth = jnp.zeros((edge, rank), jnp.float32)
        for part in range(edge // group):
            lines = slice(part * group, (part + 1) * group)
            place_at = pl.ds(part * chunk, chunk)
            right = lax.dot_general(misfit[:, place_at], pair_ab[...], (((0,), (0,)), ((), ())), preferred_element_type=jnp.float32).reshape(group, edge, rank)
            grads_ref[0, 2, lines, :] = jnp.sum(right * four[None, :, :], axis=1)
            fourth = fourth + jnp.sum(right * three[lines][:, None, :], axis=0)
        grads_ref[0, 3] = fourth


def tile_gradients(pos, count, tile_stack, blocks):
    slots, height, width = tile_stack.shape
    rank = blocks.shape[2]
    return pl.pallas_call(
        tile_kernel,
        out_shape=jax.ShapeDtypeStruct((slots, 4, TILE, rank), jnp.float32),
        grid_spec=pltpu.PrefetchScalarGridSpec(
            num_scalar_prefetch=2,
            grid=(slots,),
            in_specs=[
                pl.BlockSpec((1, height, width), lambda s, pos, count: (jnp.minimum(s, count[0] - 1), 0, 0)),
                pl.BlockSpec(memory_space=pltpu.VMEM),
            ],
            out_specs=pl.BlockSpec((1, 4, TILE, rank), lambda s, pos, count: (s, 0, 0, 0)),
            scratch_shapes=[
                pltpu.VMEM((height, rank), jnp.bfloat16),
                pltpu.VMEM((width, rank), jnp.bfloat16),
                pltpu.VMEM((height, width), jnp.bfloat16),
            ],
        ),
        compiler_params=pltpu.CompilerParams(vmem_limit_bytes=40 << 20),
        cost_estimate=pl.CostEstimate(flops=6 * slots * height * width * rank, bytes_accessed=2 * slots * height * width, transcendentals=0),
        name="tile_gradients",
    )(pos, count, tile_stack, blocks)


def reduce_kernel(tiles, rows, inverse_ref, names_ref, grads_ref, factors_ref, out_ref, packed, landed, target, gathered, send_sem, recv_sem, all_send, all_recv):
    peers = tiles * rows
    my_tile, my_row = lax.axis_index("tiles"), lax.axis_index("rows")
    me = my_tile * rows + my_row
    share = TILE // tiles
    span = CAP * share
    local = factors_ref.shape[0]
    rank = grads_ref.shape[2]
    enter(me, peers, rows)

    def message(other, slot):
        return pltpu.make_async_remote_copy(
            src_ref=packed.at[other], dst_ref=landed.at[slot], send_sem=send_sem.at[other], recv_sem=recv_sem.at[slot],
            device_id=place(other, rows), device_id_type=MESH)

    @pl.loop(0, rows)
    def _(k):
        owner = lax.rem(my_row + k, rows)
        found = []
        for spot in range(CAP):
            index = inverse_ref[0, owner * CAP + spot]
            block = grads_ref[jnp.maximum(index, 0)]
            found.append(jnp.where(index >= 0, block, 0.0))
        for tile in range(tiles):
            lines = slice(tile * share, (tile + 1) * share)
            packed[tile * rows + owner] = jnp.concatenate([block[lines] for block in found], axis=0).astype(jnp.bfloat16)

        @pl.when(k > 0)
        def _():
            message(my_tile * rows + owner, me).start()

        @pl.loop(1, tiles)
        def _(j):
            message(lax.rem(my_tile + j, tiles) * rows + owner, me).start()

    landed[me] = packed[me]
    inside = lax.broadcasted_iota(jnp.int32, (span, LANES), 0)

    @pl.loop(0, peers)
    def _(source):
        base = jnp.zeros((span, LANES), jnp.int32)
        for spot in range(CAP):
            name = names_ref[source, my_row * CAP + spot]
            line = jnp.where(name >= 0, name * share - spot * share, -(1 << 20))
            base = jnp.where(inside // share == spot, line, base)
        target[pl.ds(source * span, span), :] = base + inside

    @pl.loop(1, peers)
    def _(k):
        other = lax.rem(me + k, peers)
        message(other, other).wait_recv()

    total = local // TILE * share
    marks = [
        jnp.where(target[...] == lax.broadcasted_iota(jnp.int32, (peers * span, LANES), 1) + at, 1.0, 0.0).astype(jnp.bfloat16)
        for at in range(0, total, LANES)
    ]
    everything = landed[...].reshape(peers * span, rank)
    for at, mark in zip(range(0, total, LANES), marks):
        size = min(LANES, total - at)
        summed = lax.dot_general(mark, everything, (((0,), (0,)), ((), ())), preferred_element_type=jnp.float32)
        gathered[my_tile, pl.ds(at, size), :] = summed[:size].astype(jnp.bfloat16)

    def spread(other, slot):
        return pltpu.make_async_remote_copy(
            src_ref=gathered.at[my_tile], dst_ref=gathered.at[slot], send_sem=all_send.at[other], recv_sem=all_recv.at[slot],
            device_id=place(other * rows + my_row, rows), device_id_type=MESH)

    @pl.loop(1, tiles)
    def _(j):
        spread(lax.rem(my_tile + j, tiles), my_tile).start()

    per = 16 // share

    if share % 8 == 0:
        def update(tile):
            for at in range(0, total, 16):
                values = gathered[tile, pl.ds(at, 16), :].astype(jnp.float32)
                for piece in range(per):
                    line = pl.multiple_of((at // share + piece) * TILE + tile * share, share)
                    spot = pl.ds(line, share)
                    out_ref[spot, :] = factors_ref[spot, :] - step_size * values[piece * share:(piece + 1) * share]

        update(my_tile)

        @pl.loop(1, tiles)
        def _(j):
            other = lax.rem(my_tile + j, tiles)
            spread(other, other).wait_recv()
            update(other)
    else:
        @pl.loop(1, tiles)
        def _(j):
            other = lax.rem(my_tile + j, tiles)
            spread(other, other).wait_recv()

        for at in range(0, total, 16):
            values = [gathered[tile, pl.ds(at, 16), :].astype(jnp.float32) for tile in range(tiles)]
            for piece in range(per):
                spot = pl.ds((at // share + piece) * TILE, TILE)
                block = jnp.concatenate([value[piece * share:(piece + 1) * share] for value in values], axis=0)
                out_ref[spot, :] = factors_ref[spot, :] - step_size * block

    @pl.loop(1, tiles)
    def _(j):
        spread(lax.rem(my_tile + j, tiles), my_tile).wait_send()

    @pl.loop(1, peers)
    def _(k):
        message(lax.rem(me + k, peers), me).wait_send()


def reduce_update(inverse, names, grads, factors, tiles, rows):
    peers = tiles * rows
    local, rank = factors.shape
    share = TILE // tiles
    span = CAP * share
    total = local // TILE * share
    return pl.pallas_call(
        functools.partial(reduce_kernel, tiles, rows),
        out_shape=jax.ShapeDtypeStruct((local, rank), jnp.float32),
        in_specs=[pl.BlockSpec(memory_space=pltpu.SMEM)] * 2 + [pl.BlockSpec(memory_space=pltpu.VMEM)] * 2,
        out_specs=pl.BlockSpec(memory_space=pltpu.VMEM),
        scratch_shapes=[
            pltpu.VMEM((peers, span, rank), jnp.bfloat16),
            pltpu.VMEM((peers, span, rank), jnp.bfloat16),
            pltpu.VMEM((peers * span, LANES), jnp.int32),
            pltpu.VMEM((tiles, total, rank), jnp.bfloat16),
            pltpu.SemaphoreType.DMA((peers,)),
            pltpu.SemaphoreType.DMA((peers,)),
            pltpu.SemaphoreType.DMA((tiles,)),
            pltpu.SemaphoreType.DMA((tiles,)),
        ],
        compiler_params=pltpu.CompilerParams(collective_id=1, has_side_effects=True, vmem_limit_bytes=40 << 20),
        name="reduce_update",
    )(inverse, names, grads, factors)


def tables(coords, live_count, local_blocks):
    slots = coords.shape[0]
    names = slots * 4
    flat = coords.reshape(names)
    owner = flat // local_blocks
    order = jnp.arange(names)
    live = order // 4 < live_count
    earlier = (owner[None, :] == owner[:, None]) & live[None, :] & (order[None, :] < order[:, None])
    spot = owner * CAP + jnp.sum(earlier.astype(jnp.int32), axis=1)
    spot = jnp.where(live, spot, -1)
    hit = spot[None, :] == jnp.arange(LANES)[:, None]
    block = (order % 4) * local_blocks + flat - owner * local_blocks
    want = jnp.max(jnp.where(hit, block[None, :], -1), axis=1)
    inverse = jnp.max(jnp.where(hit, order[None, :], -1), axis=1)
    return jnp.maximum(spot, 0), want.reshape(1, LANES), inverse.reshape(1, LANES)


def on_device(tile_values, tile_coords, tile_count, factors):
    tiles, rows = lax.axis_size("tiles"), lax.axis_size("rows")
    modes, local_rows, rank = factors.shape
    spot, want, inverse = tables(tile_coords[0], tile_count[0], local_rows // TILE)
    flat = factors.reshape(modes * local_rows, rank)
    names, blocks = fetch(want, flat.reshape(-1, TILE, rank), tiles, rows)
    grads = tile_gradients(spot, tile_count, tile_values[0], blocks.reshape(rows * CAP, TILE, rank))
    slots = tile_values.shape[1]
    updated = reduce_update(inverse, names.reshape(tiles * rows, LANES), grads.reshape(slots * 4, TILE, rank), flat, tiles, rows)
    return updated.reshape(factors.shape)


def solution(mesh):
    return jax.shard_map(
        on_device,
        mesh=mesh,
        in_specs=(
            P(("tiles", "rows"), None, None, None),
            P(("tiles", "rows"), None, None),
            P(("tiles", "rows")),
            P(None, "rows", None),
        ),
        out_specs=P(None, "rows", None),
        check_vma=False,
    )
```

time: 335 us -> 75.8 us (0.23)
  the two profiles are of different devices: /device:TPU:0 before, /device:TPU:26 now
where the time goes in v1:
time: 75.8 us; the launch traced here: 74.8 us
  Pallas kernels  70.3 us (93%)
  local copies, waits for them, and re-layouts  3.39 us (4%)
    pallas_call x1, Pallas kernels, reduce_update(): pl.pallas_call(functools.partial(reduce_kernel, tiles, rows), out_shape=j...  40.6 us
    pallas_call x1, Pallas kernels, tile_gradients(): pl.pallas_call(tile_kernel, out_shape=jax.ShapeDtypeStruct((slots, 4, TIL...  16.2 us
    pallas_call x1, Pallas kernels, fetch(): pl.pallas_call(functools.partial(fetch_kernel, tiles, rows), out_shape=(j...  13.5 us
    unnamed x6, local copies, waits for them, and re-layouts  3.31 us

profile of v1, /device:TPU:26, one launch (start us, length us, event | category | flops | bytes accessed | tf_op | source)
XLA Modules:
  0.0 74.8 jit_solution(8342875916601793615)
XLA Ops:
  0.7 0.8 %copy.7 = s32[1,8,4]{2,1,0:T(8,128)S(1)} copy(s32[1,8,4]{1,2,0:T(4,128)} %param.5) | data formatting | bytes 256 | tf_op args[1]
  1.4 0.1 reshape_squeeze.3
  1.5 0.2 convert_reduce_fusion
  1.7 0.1 select_reduce_fusion
  1.8 0.0 copy-start
  1.8 1.4 %copy-done = f32[4,384,256]{2,1,0:T(8,128)S(1)} copy-done((f32[4,384,256]{2,1,0:T(8,128)S(1)}, f32[4,384,256]{2,1,0:T(8,128)}, u32[]{:S(2)}) %copy-start) | copy-done | bytes 1572888
  3.2 13.5 %fetch_blocks.1 = (s32[32,1,128]{2,1,0:T(1,128)S(1)}, bf16[8,128,256]{2,1,0:T(8,128)(2,1)S(1)}) custom-call(s32[1,128]{1,0:T(1,128)S(1)} %bitcast.18, f32[48,32,256]{2,1,0:T(8,128)S(1)} %bitcast.12), custom_call_target="tpu_custom_call" | custom-call | tf_op jit(solution)/shard_map/fetch_blocks/pallas_call | solution.py:108
  16.8 0.0 copy-start.1
  16.8 16.2 %tile_gradients.1 = f32[8,4,32,256]{3,2,1,0:T(8,128)S(1)} custom-call(s32[32]{0:T(128)S(1)} %get-tuple-element.11.pos_ref, s32[1]{0:T(128)} %copy.9.count_ref, bf16[8,1024,1024]{2,1,0:T(8,128)(2,1)} %bitcast.20, bf16[32,32,256]{2,1,0:T(8,128)(2,1)S(1)} %bitcast.19), custom_call_target="tpu_custom_call" | custom-call | flops 12884901888 | bytes 16777216 | tf_op jit(solution)/shard_map/tile_gradients/pallas_call | solution.py:169
  33.0 0.0 copy-done.1
  33.0 40.6 %reduce_update.1 = f32[1536,256]{1,0:T(8,128)S(1)} custom-call(s32[1,128]{1,0:T(1,128)S(1)} %bitcast.17, s32[32,128]{1,0:T(8,128)S(1)} %bitcast.16, f32[32,32,256]{2,1,0:T(8,128)S(1)} %bitcast.15, f32[1536,256]{1,0:T(8,128)S(1)} %bitcast.13), custom_call_target="tpu_custom_call" | custom-call | tf_op jit(solution)/shard_map/reduce_update/pallas_call | solution.py:310
  73.6 1.1 %copy.10 = f32[4,384,256]{2,1,0:T(8,128)} copy(f32[4,384,256]{2,1,0:T(8,128)S(1)} %bitcast.14) | data formatting | bytes 3145728
  (3 shorter events, 0.0 us)
Async XLA Ops:
  1.8 1.4 %copy-start = (f32[4,384,256]{2,1,0:T(8,128)S(1)}, f32[4,384,256]{2,1,0:T(8,128)}, u32[]{:S(2)}) copy-start(f32[4,384,256]{2,1,0:T(8,128)} %param.7) | copy-start | bytes 4718596
  16.8 16.2 %copy-start.1 = (f32[4,384,256]{2,1,0:T(8,128)S(1)}, f32[4,384,256]{2,1,0:T(8,128)}, u32[]{:S(2)}) copy-start(f32[4,384,256]{2,1,0:T(8,128)} %param.7) | copy-start | bytes 4718596

commit v2 on v0

v2 whole, which is shorter than its diff:
```python
import functools

import jax
import jax.numpy as jnp
from jax import lax
from jax.experimental import pallas as pl
from jax.experimental.pallas import tpu as pltpu
from jax.sharding import PartitionSpec as P

TILE = 32
CAP = 4
LANES = 128
MESH = pl.DeviceIdType.MESH

step_size = 0.02


def place(index, rows):
    return {"tiles": index // rows, "rows": lax.rem(index, rows)}


def step_kernel(
    tiles, rows, spot_ref, inverse_ref, want_ref, tile_hbm, factors_hbm, out_hbm,
    factors, stack, names, name_scalars, row_scalars, ask_packed, blocks, ab_even, ab_odd, cd_even, cd_odd, misfit_even, misfit_odd,
    grads, packed, landed, target, gathered,
    name_send, name_recv, block_send, block_recv, send_sem, recv_sem, up_send, down_send, all_recv, tile_sem, out_sem, local_sem,
):
    peers = tiles * rows
    my_tile, my_row = lax.axis_index("tiles"), lax.axis_index("rows")
    me = my_tile * rows + my_row
    slots = stack.shape[0]
    rank = factors.shape[2]
    row_place = lambda peer: my_tile * rows + peer
    far_place = lambda j, k: lax.rem(my_tile + j, tiles) * rows + lax.rem(my_row + k, rows)

    bring_factors = pltpu.make_async_copy(factors_hbm, factors, local_sem)
    bring_factors.start()
    barrier = pltpu.get_barrier_semaphore()
    for j in range(tiles):
        @pl.loop(0 if j else 1, rows, unroll=True)
        def _(k):
            pl.semaphore_signal(barrier, inc=1, device_id=place(far_place(j, k), rows), device_id_type=MESH)

    def tile_copy(slot):
        return pltpu.make_async_copy(tile_hbm.at[slot], stack.at[slot], tile_sem.at[slot])

    @pl.loop(0, slots)
    def _(slot):
        tile_copy(slot).start()

    names[me] = want_ref[...]
    bring_factors.wait()
    pl.semaphore_wait(barrier, peers - 1)

    def name_copy(other, slot):
        return pltpu.make_async_remote_copy(
            src_ref=want_ref, dst_ref=names.at[slot], send_sem=name_send.at[other], recv_sem=name_recv.at[slot],
            device_id=place(other, rows), device_id_type=MESH)

    @pl.loop(1, rows, unroll=True)
    def _(k):
        name_copy(row_place(lax.rem(my_row + k, rows)), me).start()

    @pl.loop(1, rows)
    def _(k):
        other = row_place(lax.rem(my_row + k, rows))
        name_copy(other, other).wait_recv()

    bring_names = pltpu.make_async_copy(names.at[pl.ds(my_tile * rows, rows)], row_scalars, local_sem)
    bring_names.start()
    bring_names.wait()

    def block_copy(peer, slot):
        return pltpu.make_async_remote_copy(
            src_ref=ask_packed.at[peer], dst_ref=blocks.at[slot], send_sem=block_send.at[peer], recv_sem=block_recv.at[slot],
            device_id=place(row_place(peer), rows), device_id_type=MESH)

    def read(peer, spot):
        return factors[jnp.maximum(row_scalars[peer, 0, my_row * CAP + spot], 0)].astype(jnp.bfloat16)

    @pl.loop(1, rows, unroll=True)
    def _(k):
        peer = lax.rem(my_row + k, rows)
        for spot in range(CAP):
            ask_packed[peer, spot] = read(peer, spot)
        block_copy(peer, my_row).start()

    for spot in range(CAP):
        blocks[my_row, spot] = read(my_row, spot)

    @pl.loop(1, tiles)
    def _(j):
        @pl.loop(0, rows)
        def _(k):
            name_copy(far_place(j, k), me).start()

    @pl.loop(1, rows)
    def _(k):
        peer = lax.rem(my_row + k, rows)
        block_copy(peer, peer).wait_recv()

    edge = TILE
    chunk = 256
    group = chunk // edge
    buffers = ((ab_even, cd_even, misfit_even), (ab_odd, cd_odd, misfit_odd))

    def block(slot, mode):
        index = spot_ref[0, mode * slots + slot]
        return blocks[index // CAP, lax.rem(index, CAP)].astype(jnp.float32)

    def work(slot, parity, before):
        if slot is not None:
            tile_copy(slot).wait()
            pair_ab, pair_cd, misfit = buffers[parity]
            one, two, three, four = (block(slot, mode) for mode in range(4))
            for part in range(edge // group):
                lines = slice(part * group, (part + 1) * group)
                at = pl.ds(part * chunk, chunk)
                pair_ab[at, :] = (one[lines][:, None, :] * two[None, :, :]).reshape(chunk, rank).astype(jnp.bfloat16)
                pair_cd[at, :] = (three[lines][:, None, :] * four[None, :, :]).reshape(chunk, rank).astype(jnp.bfloat16)
            second = jnp.zeros((edge, rank), jnp.float32)
        if before is not None:
            old_ab, _, old_misfit = buffers[1 - parity]
            old_three, old_four = block(before, 2), block(before, 3)
            fourth = jnp.zeros((edge, rank), jnp.float32)
        for part in range(edge // group):
            lines = slice(part * group, (part + 1) * group)
            at = pl.ds(part * chunk, chunk)
            if before is not None:
                right = lax.dot_general(old_misfit[:, at], old_ab[...], (((0,), (0,)), ((), ())), preferred_element_type=jnp.float32)
                right = right.reshape(group, edge, rank)
                grads[before * 4 + 2, lines, :] = jnp.sum(right * old_four[None, :, :], axis=1)
                fourth = fourth + jnp.sum(right * old_three[lines][:, None, :], axis=0)
            if slot is not None:
                model = lax.dot_general(pair_ab[at, :], pair_cd[...], (((1,), (1,)), ((), ())), preferred_element_type=jnp.float32)
                off = jnp.clip(model - stack[slot, at, :].astype(jnp.float32), -1.0, 1.0).astype(jnp.bfloat16)
                misfit[at, :] = off
                left = jnp.dot(off, pair_cd[...], preferred_element_type=jnp.float32).reshape(group, edge, rank)
                grads[slot * 4, lines, :] = jnp.sum(left * two[None, :, :], axis=1)
                second = second + jnp.sum(left * one[lines][:, None, :], axis=0)
        if slot is not None:
            grads[slot * 4 + 1] = second
        if before is not None:
            grads[before * 4 + 3] = fourth

    work(0, 0, None)

    @pl.loop(0, (slots - 1) // 2)
    def _(i):
        work(2 * i + 1, 1, 2 * i)
        work(2 * i + 2, 0, 2 * i + 1)

    if slots % 2 == 0:
        work(slots - 1, 1, slots - 2)
    work(None, slots % 2, slots - 1)

    share = TILE // tiles
    span = CAP * share
    total = factors.shape[0] * share

    def message(other, slot):
        return pltpu.make_async_remote_copy(
            src_ref=packed.at[other], dst_ref=landed.at[slot], send_sem=send_sem.at[other], recv_sem=recv_sem.at[slot],
            device_id=place(other, rows), device_id_type=MESH)

    @pl.loop(0, rows)
    def _(k):
        owner = lax.rem(my_row + k, rows)
        found = []
        for spot in range(CAP):
            index = inverse_ref[0, owner * CAP + spot]
            found.append(jnp.where(index >= 0, grads[jnp.maximum(index, 0)], 0.0))
        for tile in range(tiles):
            lines = slice(tile * share, (tile + 1) * share)
            packed[tile * rows + owner] = jnp.concatenate([piece[lines] for piece in found], axis=0).astype(jnp.bfloat16)

        for j in range(1, tiles):
            message(lax.rem(my_tile + j, tiles) * rows + owner, me).start()

        @pl.when(k > 0)
        def _():
            message(row_place(owner), me).start()

    landed[me] = packed[me]

    @pl.loop(1, tiles)
    def _(j):
        @pl.loop(0, rows)
        def _(k):
            other = far_place(j, k)
            name_copy(other, other).wait_recv()

    bring_all = pltpu.make_async_copy(names, name_scalars, local_sem)
    bring_all.start()
    bring_all.wait()
    inside = lax.broadcasted_iota(jnp.int32, (span, LANES), 0)

    @pl.loop(0, peers)
    def _(source):
        base = jnp.zeros((span, LANES), jnp.int32)
        for spot in range(CAP):
            name = name_scalars[source, 0, my_row * CAP + spot]
            line = jnp.where(name >= 0, name * share - spot * share, -(1 << 20))
            base = jnp.where(inside // share == spot, line, base)
        target[pl.ds(source * span, span), :] = base + inside

    marks = [
        jnp.where(target[...] == lax.broadcasted_iota(jnp.int32, (peers * span, LANES), 1) + at, 1.0, 0.0).astype(jnp.bfloat16)
        for at in range(0, total, LANES)
    ]

    @pl.loop(1, peers)
    def _(k):
        other = lax.rem(me + k, peers)
        message(other, other).wait_recv()

    everything = landed[...].reshape(peers * span, rank)
    for at, mark in zip(range(0, total, LANES), marks):
        size = min(LANES, total - at)
        summed = lax.dot_general(mark, everything, (((0,), (0,)), ((), ())), preferred_element_type=jnp.float32)
        gathered[my_tile, pl.ds(at, size), :] = summed[:size].astype(jnp.bfloat16)

    def spread(towards, share_at, sems):
        return pltpu.make_async_remote_copy(
            src_ref=gathered.at[share_at], dst_ref=gathered.at[share_at], send_sem=sems.at[share_at], recv_sem=all_recv.at[share_at],
            device_id=place(towards * rows + my_row, rows), device_id_type=MESH)

    def each_way(tile, act):
        @pl.when((tile <= my_tile) & (my_tile + 1 < tiles))
        def _():
            act(spread(my_tile + 1, tile, up_send))

        @pl.when((tile >= my_tile) & (my_tile > 0))
        def _():
            act(spread(my_tile - 1, tile, down_send))

    per = 16 // share

    def finished(tile):
        lines = pl.ds(pl.multiple_of(tile * share, share), share)
        return pltpu.make_async_copy(factors.at[:, lines, :], out_hbm.at[:, lines, :], out_sem.at[tile])

    def update(tile):
        if share % 8:
            return
        lines = pl.ds(pl.multiple_of(tile * share, share), share)
        for at in range(0, total, 16):
            values = gathered[tile, pl.ds(at, 16), :].astype(jnp.float32)
            for piece in range(per):
                name = at // share + piece
                factors[name, lines, :] = factors[name, lines, :] - step_size * values[piece * share:(piece + 1) * share]
        finished(tile).start()

    each_way(my_tile, lambda copy: copy.start())
    update(my_tile)

    for away in range(1, tiles):
        for tile, inside_chain in ((my_tile - away, my_tile >= away), (my_tile + away, my_tile + away < tiles)):
            @pl.when(inside_chain)
            def _():
                spread(my_tile, tile, up_send).wait_recv()
                each_way(tile, lambda copy: copy.start())
                update(tile)

    if share % 8:
        for at in range(0, total, 16):
            values = [gathered[tile, pl.ds(at, 16), :].astype(jnp.float32) for tile in range(tiles)]
            for piece in range(per):
                name = at // share + piece
                whole = jnp.concatenate([value[piece * share:(piece + 1) * share] for value in values], axis=0)
                factors[name] = factors[name] - step_size * whole
        write = pltpu.make_async_copy(factors, out_hbm, local_sem)
        write.start()
        write.wait()
    else:
        @pl.loop(0, tiles)
        def _(tile):
            finished(tile).wait()

    @pl.loop(0, tiles)
    def _(tile):
        each_way(tile, lambda copy: copy.wait_send())

    @pl.loop(1, rows)
    def _(k):
        peer = lax.rem(my_row + k, rows)
        block_copy(peer, my_row).wait_send()

    @pl.loop(1, peers)
    def _(k):
        other = lax.rem(me + k, peers)
        name_copy(other, me).wait_send()
        message(other, me).wait_send()


def step(spot, inverse, want, tile_stack, factors, tiles, rows):
    peers = tiles * rows
    slots, height, width = tile_stack.shape
    local, edge, rank = factors.shape
    share = TILE // tiles
    span = CAP * share
    dma = lambda *shape: pltpu.SemaphoreType.DMA(shape)
    bf16 = lambda *shape: pltpu.VMEM(shape, jnp.bfloat16)
    return pl.pallas_call(
        functools.partial(step_kernel, tiles, rows),
        out_shape=jax.ShapeDtypeStruct((local, edge, rank), jnp.float32),
        in_specs=[pl.BlockSpec(memory_space=pltpu.SMEM)] * 2 + [pl.BlockSpec(memory_space=pltpu.VMEM)] + [pl.BlockSpec(memory_space=pl.ANY)] * 2,
        out_specs=pl.BlockSpec(memory_space=pl.ANY),
        scratch_shapes=[
            pltpu.VMEM((local, edge, rank), jnp.float32),
            bf16(slots, height, width),
            pltpu.VMEM((peers, 1, LANES), jnp.int32),
            pltpu.SMEM((peers, 1, LANES), jnp.int32),
            pltpu.SMEM((rows, 1, LANES), jnp.int32),
            bf16(rows, CAP, TILE, rank),
            bf16(rows, CAP, TILE, rank),
            bf16(height, rank), bf16(height, rank), bf16(width, rank), bf16(width, rank),
            bf16(height, width), bf16(height, width),
            pltpu.VMEM((slots * 4, TILE, rank), jnp.float32),
            bf16(peers, span, rank),
            bf16(peers, span, rank),
            pltpu.VMEM((peers * span, LANES), jnp.int32),
            bf16(tiles, local * share, rank),
            dma(peers), dma(peers), dma(rows), dma(rows), dma(peers), dma(peers),
            dma(tiles), dma(tiles), dma(tiles), dma(slots), dma(tiles), pltpu.SemaphoreType.DMA,
        ],
        compiler_params=pltpu.CompilerParams(collective_id=0, has_side_effects=True, vmem_limit_bytes=56 << 20),
        cost_estimate=pl.CostEstimate(flops=6 * slots * height * width * rank, bytes_accessed=2 * slots * height * width, transcendentals=0),
        name="gradient_step",
    )(spot, inverse, want, tile_stack, factors)


def tables(coords, live_count, local_blocks):
    slots = coords.shape[0]
    names = slots * 4
    flat = coords.T.reshape(names)
    owner = flat // local_blocks
    order = jnp.arange(names)
    live = order % slots < live_count
    earlier = (owner[None, :] == owner[:, None]) & live[None, :] & (order[None, :] < order[:, None])
    spot = owner * CAP + jnp.sum(earlier.astype(jnp.int32), axis=1)
    spot = jnp.where(live, spot, -1)
    hit = spot[None, :] == jnp.arange(LANES)[:, None]
    block = (order // slots) * local_blocks + flat - owner * local_blocks
    want = jnp.max(jnp.where(hit, block[None, :], -1), axis=1)
    inverse = jnp.max(jnp.where(hit, ((order % slots) * 4 + order // slots)[None, :], -1), axis=1)
    return jnp.maximum(spot, 0).reshape(1, names), want.reshape(1, LANES), inverse.reshape(1, LANES)


def on_device(tile_values, tile_coords, tile_count, factors):
    tiles, rows = lax.axis_size("tiles"), lax.axis_size("rows")
    modes, local_rows, rank = factors.shape
    spot, want, inverse = tables(tile_coords[0], tile_count[0], local_rows // TILE)
    updated = step(spot, inverse, want, tile_values[0], factors.reshape(-1, TILE, rank), tiles, rows)
    return updated.reshape(factors.shape)


def solution(mesh):
    return jax.shard_map(
        on_device,
        mesh=mesh,
        in_specs=(
            P(("tiles", "rows"), None, None, None),
            P(("tiles", "rows"), None, None),
            P(("tiles", "rows")),
            P(None, "rows", None),
        ),
        out_specs=P(None, "rows", None),
        check_vma=False,
    )
```

time: 335 us -> 77 us (0.23)
  waiting for transfers between devices: 240 us -> 0 us
  Pallas kernels: 0 us -> 69.7 us
  matrix products: 26.9 us -> 0 us
  local copies, waits for them, and re-layouts: 27.5 us -> 3.59 us
  other arithmetic: 22.2 us -> 2.82 us
  between operations: 13.2 us -> 0.67 us
  loops' own time: 4.18 us -> 0 us
    reduce_scatter x1 -> x0, waiting for transfers between devices: 120 us -> none  [on_device(): lax.psum_scatter(dense_grads, 'rows', scatter_dimension=1, tiled=True)]
    psum x1 -> x0, waiting for transfers between devices: 71.5 us -> none  [on_device(): total_grad = lax.psum(partial_sum, 'tiles')]
    pallas_call x0 -> x1, Pallas kernels: none -> 69.7 us  [step(): pl.pallas_call(functools.partial(step_kernel, tiles, rows), out_shape=jax...]
    all_gather x1 -> x0, waiting for transfers between devices: 47.9 us -> none  [on_device(): everything = lax.all_gather(narrow, 'rows', axis=1, tiled=True)]
    dot_general x15 -> x0, matrix products: 26.9 us -> none  [the longest x5 11.7 us: tile_grads(): lax.dot_general(pair_ab, pair_cd, (((1,), (1,)), ((), ())), preferred_ele...]
    gather x1 -> x0, local copies, waits for them, and re-layouts: 13.2 us -> none  [on_device(): blocks = everything[mode_index, row_index]]
    dot_general x5 -> x0, local copies, waits for them, and re-layouts: 12.9 us -> none  [tile_grads(): lax.dot_general(misfit, pair_ab, (((0,), (0,)), ((), ())), preferred_elem...]
    unnamed x4 -> x0, other arithmetic: 12.1 us -> none
  transfers between devices with their start and end apart: 3 -> 0, of which waited for: 3 -> 0; matrix products, arithmetic and copies ran while one was open for 0% -> 0% of each run, Pallas kernels for 0% -> 0%
where the time goes in v2:
time: 77 us; the launch traced here: 76.8 us
  Pallas kernels  69.7 us (91%)
  local copies, waits for them, and re-layouts  3.59 us (5%)
  other arithmetic  2.82 us (4%)
    pallas_call x1, Pallas kernels, step(): pl.pallas_call(functools.partial(step_kernel, tiles, rows), out_shape=jax...  69.7 us
    unnamed x1, local copies, waits for them, and re-layouts  2.65 us

profile of v2, /device:TPU:0, one launch (start us, length us, event | category | flops | bytes accessed | tf_op | source)
XLA Modules:
  0.0 76.8 jit_solution(4879977527999757908)
XLA Ops:
  0.7 0.8 reshape.180
  1.4 0.7 fusion.1
  2.1 0.1 and.101
  2.2 0.2 convert_reduce_fusion
  2.4 0.7 select_reduce_fusion
  3.1 0.7 broadcast_divide_fusion
  3.8 0.1 div.42
  3.9 0.6 fusion.4.spot_ref
  4.4 69.7 %gradient_step.1 = f32[48,32,256]{2,1,0:T(8,128)} custom-call(s32[1,32]{1,0:T(1,128)} %fusion.4.spot_ref, s32[1,128]{1,0:T(1,128)} %bitcast.21, s32[1,128]{1,0:T(1,128)} %bitcast.20, bf16[8,1024,1024]{2,1,0:T(8,128)(2,1)} %bitcast.22, f32[48,32,256]{2,1,0:T(8,128)} %bitcast.23), custom_call_target="tpu_custom_call" | custom-call | flops 12884901888 | bytes 16777216 | tf_op jit(solution)/shard_map/gradient_step/pallas_call | solution.py:304
  74.1 2.7 %copy.7 = f32[4,384,256]{2,1,0:T(8,128)} copy(f32[4,384,256]{2,1,0:T(8,128)} %bitcast.18) | data formatting | bytes 3145728
  (3 shorter events, 0.0 us)

commit v3 on v2

--- a/solution.py
+++ b/solution.py
@@ -20,10 +20,10 @@
 
 
 def step_kernel(
-    tiles, rows, spot_ref, inverse_ref, want_ref, tile_hbm, factors_hbm, out_hbm,
-    factors, stack, names, name_scalars, row_scalars, ask_packed, blocks, ab_even, ab_odd, cd_even, cd_odd, misfit_even, misfit_odd,
+    tiles, rows, spot_ref, inverse_ref, want_ref, tile_hbm, factors_hbm, out_ref,
+    factors, stack, names, name_scalars, row_scalars, ask_packed, blocks, pair_ab, pair_cd, misfit,
     grads, packed, landed, target, gathered,
-    name_send, name_recv, block_send, block_recv, send_sem, recv_sem, up_send, down_send, all_recv, tile_sem, out_sem, local_sem,
+    name_send, name_recv, block_send, block_recv, send_sem, recv_sem, up_send, down_send, all_recv, tile_sem, local_sem,
 ):
     peers = tiles * rows
     my_tile, my_row = lax.axis_index("tiles"), lax.axis_index("rows")
@@ -44,10 +44,6 @@
     def tile_copy(slot):
         return pltpu.make_async_copy(tile_hbm.at[slot], stack.at[slot], tile_sem.at[slot])
 
-    @pl.loop(0, slots)
-    def _(slot):
-        tile_copy(slot).start()
-
     names[me] = want_ref[...]
     bring_factors.wait()
     pl.semaphore_wait(barrier, peers - 1)
@@ -94,6 +90,9 @@
         def _(k):
             name_copy(far_place(j, k), me).start()
 
+    tile_copy(0).start()
+    tile_copy(1).start()
+
     @pl.loop(1, rows)
     def _(k):
         peer = lax.rem(my_row + k, rows)
@@ -102,57 +101,43 @@
     edge = TILE
     chunk = 256
     group = chunk // edge
-    buffers = ((ab_even, cd_even, misfit_even), (ab_odd, cd_odd, misfit_odd))
-
     def block(slot, mode):
-        index = spot_ref[0, mode * slots + slot]
+        index = spot_ref[slot * 4 + mode]
         return blocks[index // CAP, lax.rem(index, CAP)].astype(jnp.float32)
 
-    def work(slot, parity, before):
-        if slot is not None:
-            tile_copy(slot).wait()
-            pair_ab, pair_cd, misfit = buffers[parity]
-            one, two, three, four = (block(slot, mode) for mode in range(4))
-            for part in range(edge // group):
-                lines = slice(part * group, (part + 1) * group)
-                at = pl.ds(part * chunk, chunk)
-                pair_ab[at, :] = (one[lines][:, None, :] * two[None, :, :]).reshape(chunk, rank).astype(jnp.bfloat16)
-                pair_cd[at, :] = (three[lines][:, None, :] * four[None, :, :]).reshape(chunk, rank).astype(jnp.bfloat16)
-            second = jnp.zeros((edge, rank), jnp.float32)
-        if before is not None:
-            old_ab, _, old_misfit = buffers[1 - parity]
-            old_three, old_four = block(before, 2), block(before, 3)
-            fourth = jnp.zeros((edge, rank), jnp.float32)
+    @pl.loop(0, slots)
+    def _(slot):
+        @pl.when(slot + 2 < slots)
+        def _():
+            tile_copy(slot + 2).start()
+
+        one, two, three, four = (block(slot, mode) for mode in range(4))
         for part in range(edge // group):
             lines = slice(part * group, (part + 1) * group)
             at = pl.ds(part * chunk, chunk)
-            if before is not None:
-                right = lax.dot_general(old_misfit[:, at], old_ab[...], (((0,), (0,)), ((), ())), preferred_element_type=jnp.float32)
-                right = right.reshape(group, edge, rank)
-                grads[before * 4 + 2, lines, :] = jnp.sum(right * old_four[None, :, :], axis=1)
-                fourth = fourth + jnp.sum(right * old_three[lines][:, None, :], axis=0)
-            if slot is not None:
-                model = lax.dot_general(pair_ab[at, :], pair_cd[...], (((1,), (1,)), ((), ())), preferred_element_type=jnp.float32)
-                off = jnp.clip(model - stack[slot, at, :].astype(jnp.float32), -1.0, 1.0).astype(jnp.bfloat16)
-                misfit[at, :] = off
-                left = jnp.dot(off, pair_cd[...], preferred_element_type=jnp.float32).reshape(group, edge, rank)
-                grads[slot * 4, lines, :] = jnp.sum(left * two[None, :, :], axis=1)
-                second = second + jnp.sum(left * one[lines][:, None, :], axis=0)
-        if slot is not None:
-            grads[slot * 4 + 1] = second
-        if before is not None:
-            grads[before * 4 + 3] = fourth
-
-    work(0, 0, None)
-
-    @pl.loop(0, (slots - 1) // 2)
-    def _(i):
-        work(2 * i + 1, 1, 2 * i)
-        work(2 * i + 2, 0, 2 * i + 1)
-
-    if slots % 2 == 0:
-        work(slots - 1, 1, slots - 2)
-    work(None, slots % 2, slots - 1)
+            pair_ab[at, :] = (one[lines][:, None, :] * two[None, :, :]).reshape(chunk, rank).astype(jnp.bfloat16)
+            pair_cd[at, :] = (three[lines][:, None, :] * four[None, :, :]).reshape(chunk, rank).astype(jnp.bfloat16)
+        tile_copy(slot).wait()
+        second = jnp.zeros((edge, rank), jnp.float32)
+        for part in range(edge // group):
+            lines = slice(part * group, (part + 1) * group)
+            at = pl.ds(part * chunk, chunk)
+            model = lax.dot_general(pair_ab[at, :], pair_cd[...], (((1,), (1,)), ((), ())), preferred_element_type=jnp.float32)
+            off = jnp.clip(model - stack[slot, at, :].astype(jnp.float32), -1.0, 1.0).astype(jnp.bfloat16)
+            misfit[at, :] = off
+            left = jnp.dot(off, pair_cd[...], preferred_element_type=jnp.float32).reshape(group, edge, rank)
+            grads[slot * 4, lines, :] = jnp.sum(left * two[None, :, :], axis=1)
+            second = second + jnp.sum(left * one[lines][:, None, :], axis=0)
+        grads[slot * 4 + 1] = second
+        fourth = jnp.zeros((edge, rank), jnp.float32)
+        for part in range(edge // group):
+            lines = slice(part * group, (part + 1) * group)
+            at = pl.ds(part * chunk, chunk)
+            right = lax.dot_general(misfit[:, at], pair_ab[...], (((0,), (0,)), ((), ())), preferred_element_type=jnp.float32)
+            right = right.reshape(group, edge, rank)
+            grads[slot * 4 + 2, lines, :] = jnp.sum(right * four[None, :, :], axis=1)
+            fourth = fourth + jnp.sum(right * three[lines][:, None, :], axis=0)
+        grads[slot * 4 + 3] = fourth
 
     share = TILE // tiles
     span = CAP * share
@@ -236,30 +221,32 @@
 
     per = 16 // share
 
-    def finished(tile):
-        lines = pl.ds(pl.multiple_of(tile * share, share), share)
-        return pltpu.make_async_copy(factors.at[:, lines, :], out_hbm.at[:, lines, :], out_sem.at[tile])
-
     def update(tile):
         if share % 8:
             return
         lines = pl.ds(pl.multiple_of(tile * share, share), share)
-        for at in range(0, total, 16):
-            values = gathered[tile, pl.ds(at, 16), :].astype(jnp.float32)
+
+        @pl.loop(0, total // 16, unroll=4)
+        def _(i):
+            values = gathered[tile, pl.ds(pl.multiple_of(i * 16, 16), 16), :].astype(jnp.float32)
             for piece in range(per):
-                name = at // share + piece
-                factors[name, lines, :] = factors[name, lines, :] - step_size * values[piece * share:(piece + 1) * share]
-        finished(tile).start()
+                name = i * per + piece
+                out_ref[name, lines, :] = factors[name, lines, :] - step_size * values[piece * share:(piece + 1) * share]
 
     each_way(my_tile, lambda copy: copy.start())
     update(my_tile)
 
     for away in range(1, tiles):
-        for tile, inside_chain in ((my_tile - away, my_tile >= away), (my_tile + away, my_tile + away < tiles)):
+        both = ((my_tile - away, my_tile >= away), (my_tile + away, my_tile + away < tiles))
+        for tile, inside_chain in both:
             @pl.when(inside_chain)
             def _():
                 spread(my_tile, tile, up_send).wait_recv()
                 each_way(tile, lambda copy: copy.start())
+
+        for tile, inside_chain in both:
+            @pl.when(inside_chain)
+            def _():
                 update(tile)
 
     if share % 8:
@@ -268,14 +255,7 @@
             for piece in range(per):
                 name = at // share + piece
                 whole = jnp.concatenate([value[piece * share:(piece + 1) * share] for value in values], axis=0)
-                factors[name] = factors[name] - step_size * whole
-        write = pltpu.make_async_copy(factors, out_hbm, local_sem)
-        write.start()
-        write.wait()
-    else:
-        @pl.loop(0, tiles)
-        def _(tile):
-            finished(tile).wait()
+                out_ref[name] = factors[name] - step_size * whole
 
     @pl.loop(0, tiles)
     def _(tile):
@@ -304,8 +284,8 @@
     return pl.pallas_call(
         functools.partial(step_kernel, tiles, rows),
         out_shape=jax.ShapeDtypeStruct((local, edge, rank), jnp.float32),
-        in_specs=[pl.BlockSpec(memory_space=pltpu.SMEM)] * 2 + [pl.BlockSpec(memory_space=pltpu.VMEM)] + [pl.BlockSpec(memory_space=pl.ANY)] * 2,
-        out_specs=pl.BlockSpec(memory_space=pl.ANY),
+        in_specs=[pl.BlockSpec(memory_space=pltpu.SMEM)] * 2 + [pl.BlockSpec(memory_space=pltpu.VMEM)] + [pl.BlockSpec(memory_space=pltpu.HBM)] * 2,
+        out_specs=pl.BlockSpec(memory_space=pltpu.VMEM),
         scratch_shapes=[
             pltpu.VMEM((local, edge, rank), jnp.float32),
             bf16(slots, height, width),
@@ -314,17 +294,16 @@
             pltpu.SMEM((rows, 1, LANES), jnp.int32),
             bf16(rows, CAP, TILE, rank),
             bf16(rows, CAP, TILE, rank),
-            bf16(height, rank), bf16(height, rank), bf16(width, rank), bf16(width, rank),
-            bf16(height, width), bf16(height, width),
+            bf16(height, rank), bf16(width, rank), bf16(height, width),
             pltpu.VMEM((slots * 4, TILE, rank), jnp.float32),
             bf16(peers, span, rank),
             bf16(peers, span, rank),
             pltpu.VMEM((peers * span, LANES), jnp.int32),
             bf16(tiles, local * share, rank),
             dma(peers), dma(peers), dma(rows), dma(rows), dma(peers), dma(peers),
-            dma(tiles), dma(tiles), dma(tiles), dma(slots), dma(tiles), pltpu.SemaphoreType.DMA,
+            dma(tiles), dma(tiles), dma(tiles), dma(slots), pltpu.SemaphoreType.DMA,
         ],
-        compiler_params=pltpu.CompilerParams(collective_id=0, has_side_effects=True, vmem_limit_bytes=56 << 20),
+        compiler_params=pltpu.CompilerParams(collective_id=0, has_side_effects=True, vmem_limit_bytes=40 << 20),
         cost_estimate=pl.CostEstimate(flops=6 * slots * height * width * rank, bytes_accessed=2 * slots * height * width, transcendentals=0),
         name="gradient_step",
     )(spot, inverse, want, tile_stack, factors)
@@ -333,18 +312,18 @@
 def tables(coords, live_count, local_blocks):
     slots = coords.shape[0]
     names = slots * 4
-    flat = coords.T.reshape(names)
+    flat = coords.reshape(names)
     owner = flat // local_blocks
     order = jnp.arange(names)
-    live = order % slots < live_count
+    live = order // 4 < live_count
     earlier = (owner[None, :] == owner[:, None]) & live[None, :] & (order[None, :] < order[:, None])
     spot = owner * CAP + jnp.sum(earlier.astype(jnp.int32), axis=1)
     spot = jnp.where(live, spot, -1)
     hit = spot[None, :] == jnp.arange(LANES)[:, None]
-    block = (order // slots) * local_blocks + flat - owner * local_blocks
+    block = (order % 4) * local_blocks + flat - owner * local_blocks
     want = jnp.max(jnp.where(hit, block[None, :], -1), axis=1)
-    inverse = jnp.max(jnp.where(hit, ((order % slots) * 4 + order // slots)[None, :], -1), axis=1)
-    return jnp.maximum(spot, 0).reshape(1, names), want.reshape(1, LANES), inverse.reshape(1, LANES)
+    inverse = jnp.max(jnp.where(hit, order[None, :], -1), axis=1)
+    return jnp.maximum(spot, 0), want.reshape(1, LANES), inverse.reshape(1, LANES)
 
 
 def on_device(tile_values, tile_coords, tile_count, factors):

time: 77 us -> 73.8 us (0.958)
  other arithmetic: 2.82 us -> 0.31 us
    unnamed x1 -> x4, local copies, waits for them, and re-layouts: 2.65 us -> 3.31 us
where the time goes in v3:
time: 73.8 us; the launch traced here: 73.6 us
  Pallas kernels  69.2 us (94%)
  local copies, waits for them, and re-layouts  3.39 us (5%)
    pallas_call x1, Pallas kernels, step(): pl.pallas_call(functools.partial(step_kernel, tiles, rows), out_shape=jax...  69.2 us
    unnamed x4, local copies, waits for them, and re-layouts  3.31 us

profile of v3, /device:TPU:0, one launch (start us, length us, event | category | flops | bytes accessed | tf_op | source)
XLA Modules:
  0.0 73.6 jit_solution(10715996861826847533)
XLA Ops:
  0.7 0.8 %copy.7 = s32[1,8,4]{2,1,0:T(8,128)S(1)} copy(s32[1,8,4]{1,2,0:T(4,128)} %param.5) | data formatting | bytes 256 | tf_op args[1]
  1.4 0.1 reshape_squeeze.3
  1.5 0.2 convert_reduce_fusion
  1.7 0.1 select_reduce_fusion
  1.8 0.0 copy-start
  1.8 1.4 %copy-done = f32[4,384,256]{2,1,0:T(8,128)S(1)} copy-done((f32[4,384,256]{2,1,0:T(8,128)S(1)}, f32[4,384,256]{2,1,0:T(8,128)}, u32[]{:S(2)}) %copy-start) | copy-done | bytes 1572888
  3.2 69.2 %gradient_step.1 = f32[48,32,256]{2,1,0:T(8,128)S(1)} custom-call(s32[32]{0:T(128)S(1)} %get-tuple-element.9.spot_ref, s32[1,128]{1,0:T(1,128)S(1)} %bitcast.10, s32[1,128]{1,0:T(1,128)S(1)} %bitcast.9, bf16[8,1024,1024]{2,1,0:T(8,128)(2,1)} %bitcast.12, f32[48,32,256]{2,1,0:T(8,128)S(1)} %bitcast.11), custom_call_target="tpu_custom_call" | custom-call | flops 12884901888 | bytes 16777216 | tf_op jit(solution)/shard_map/gradient_step/pallas_call | solution.py:284
  72.4 1.1 %copy.10 = f32[4,384,256]{2,1,0:T(8,128)} copy(f32[4,384,256]{2,1,0:T(8,128)S(1)} %bitcast.8) | data formatting | bytes 3145728
  (3 shorter events, 0.0 us)
Async XLA Ops:
  1.8 1.4 %copy-start = (f32[4,384,256]{2,1,0:T(8,128)S(1)}, f32[4,384,256]{2,1,0:T(8,128)}, u32[]{:S(2)}) copy-start(f32[4,384,256]{2,1,0:T(8,128)} %param.7) | copy-start | bytes 4718596

commit v4 on v3

--- a/solution.py
+++ b/solution.py
@@ -20,10 +20,10 @@
 
 
 def step_kernel(
-    tiles, rows, spot_ref, inverse_ref, want_ref, tile_hbm, factors_hbm, out_ref,
-    factors, stack, names, name_scalars, row_scalars, ask_packed, blocks, pair_ab, pair_cd, misfit,
+    tiles, rows, spot_ref, inverse_ref, want_ref, tile_hbm, factors, out_ref,
+    stack, names, name_scalars, row_scalars, ask_packed, blocks, pair_ab, pair_cd, misfit,
     grads, packed, landed, target, gathered,
-    name_send, name_recv, block_send, block_recv, send_sem, recv_sem, up_send, down_send, all_recv, tile_sem, local_sem,
+    name_send, name_recv, block_send, block_recv, send_sem, recv_sem, direct_send, relay_send, all_recv, tile_sem, local_sem,
 ):
     peers = tiles * rows
     my_tile, my_row = lax.axis_index("tiles"), lax.axis_index("rows")
@@ -33,8 +33,6 @@
     row_place = lambda peer: my_tile * rows + peer
     far_place = lambda j, k: lax.rem(my_tile + j, tiles) * rows + lax.rem(my_row + k, rows)
 
-    bring_factors = pltpu.make_async_copy(factors_hbm, factors, local_sem)
-    bring_factors.start()
     barrier = pltpu.get_barrier_semaphore()
     for j in range(tiles):
         @pl.loop(0 if j else 1, rows, unroll=True)
@@ -45,7 +43,6 @@
         return pltpu.make_async_copy(tile_hbm.at[slot], stack.at[slot], tile_sem.at[slot])
 
     names[me] = want_ref[...]
-    bring_factors.wait()
     pl.semaphore_wait(barrier, peers - 1)
 
     def name_copy(other, slot):
@@ -102,7 +99,7 @@
     chunk = 256
     group = chunk // edge
     def block(slot, mode):
-        index = spot_ref[slot * 4 + mode]
+        index = spot_ref[mode, slot]
         return blocks[index // CAP, lax.rem(index, CAP)].astype(jnp.float32)
 
     @pl.loop(0, slots)
@@ -207,17 +204,29 @@
 
     def spread(towards, share_at, sems):
         return pltpu.make_async_remote_copy(
-            src_ref=gathered.at[share_at], dst_ref=gathered.at[share_at], send_sem=sems.at[share_at], recv_sem=all_recv.at[share_at],
+            src_ref=gathered.at[share_at], dst_ref=gathered.at[share_at], send_sem=sems, recv_sem=all_recv.at[share_at],
             device_id=place(towards * rows + my_row, rows), device_id_type=MESH)
 
-    def each_way(tile, act):
-        @pl.when((tile <= my_tile) & (my_tile + 1 < tiles))
+    last = tiles - 1
+
+    def each_direct(act):
+        for away in range(last - 1, 0, -1):
+            @pl.when(my_tile + away < tiles)
+            def _():
+                act(spread(my_tile + away, my_tile, direct_send.at[my_tile + away]))
+
+            @pl.when(my_tile >= away)
+            def _():
+                act(spread(my_tile - away, my_tile, direct_send.at[my_tile - away]))
+
+    def each_relay(tile, act):
+        @pl.when((tile == 0) & (my_tile == last - 1))
         def _():
-            act(spread(my_tile + 1, tile, up_send))
-
-        @pl.when((tile >= my_tile) & (my_tile > 0))
+            act(spread(last, 0, relay_send.at[0]))
+
+        @pl.when((tile == last) & (my_tile == 1))
         def _():
-            act(spread(my_tile - 1, tile, down_send))
+            act(spread(0, last, relay_send.at[1]))
 
     per = 16 // share
 
@@ -233,16 +242,16 @@
                 name = i * per + piece
                 out_ref[name, lines, :] = factors[name, lines, :] - step_size * values[piece * share:(piece + 1) * share]
 
-    each_way(my_tile, lambda copy: copy.start())
+    each_direct(lambda copy: copy.start())
     update(my_tile)
 
-    for away in range(1, tiles):
+    for away in (2, 1) + tuple(range(3, tiles)):
         both = ((my_tile - away, my_tile >= away), (my_tile + away, my_tile + away < tiles))
         for tile, inside_chain in both:
             @pl.when(inside_chain)
             def _():
-                spread(my_tile, tile, up_send).wait_recv()
-                each_way(tile, lambda copy: copy.start())
+                spread(my_tile, tile, direct_send.at[my_tile]).wait_recv()
+                each_relay(tile, lambda copy: copy.start())
 
         for tile, inside_chain in both:
             @pl.when(inside_chain)
@@ -257,9 +266,9 @@
                 whole = jnp.concatenate([value[piece * share:(piece + 1) * share] for value in values], axis=0)
                 out_ref[name] = factors[name] - step_size * whole
 
-    @pl.loop(0, tiles)
-    def _(tile):
-        each_way(tile, lambda copy: copy.wait_send())
+    each_direct(lambda copy: copy.wait_send())
+    each_relay(0, lambda copy: copy.wait_send())
+    each_relay(last, lambda copy: copy.wait_send())
 
     @pl.loop(1, rows)
     def _(k):
@@ -284,10 +293,9 @@
     return pl.pallas_call(
         functools.partial(step_kernel, tiles, rows),
         out_shape=jax.ShapeDtypeStruct((local, edge, rank), jnp.float32),
-        in_specs=[pl.BlockSpec(memory_space=pltpu.SMEM)] * 2 + [pl.BlockSpec(memory_space=pltpu.VMEM)] + [pl.BlockSpec(memory_space=pltpu.HBM)] * 2,
+        in_specs=[pl.BlockSpec(memory_space=pltpu.SMEM)] * 2 + [pl.BlockSpec(memory_space=pltpu.VMEM), pl.BlockSpec(memory_space=pl.ANY), pl.BlockSpec(memory_space=pltpu.VMEM)],
         out_specs=pl.BlockSpec(memory_space=pltpu.VMEM),
         scratch_shapes=[
-            pltpu.VMEM((local, edge, rank), jnp.float32),
             bf16(slots, height, width),
             pltpu.VMEM((peers, 1, LANES), jnp.int32),
             pltpu.SMEM((peers, 1, LANES), jnp.int32),
@@ -301,7 +309,7 @@
             pltpu.VMEM((peers * span, LANES), jnp.int32),
             bf16(tiles, local * share, rank),
             dma(peers), dma(peers), dma(rows), dma(rows), dma(peers), dma(peers),
-            dma(tiles), dma(tiles), dma(tiles), dma(slots), pltpu.SemaphoreType.DMA,
+            dma(tiles), dma(2), dma(tiles), dma(slots), pltpu.SemaphoreType.DMA,
         ],
         compiler_params=pltpu.CompilerParams(collective_id=0, has_side_effects=True, vmem_limit_bytes=40 << 20),
         cost_estimate=pl.CostEstimate(flops=6 * slots * height * width * rank, bytes_accessed=2 * slots * height * width, transcendentals=0),
@@ -310,19 +318,19 @@
 
 
 def tables(coords, live_count, local_blocks):
-    slots = coords.shape[0]
-    names = slots * 4
-    flat = coords.reshape(names)
+    flat = coords.T
     owner = flat // local_blocks
-    order = jnp.arange(names)
-    live = order // 4 < live_count
-    earlier = (owner[None, :] == owner[:, None]) & live[None, :] & (order[None, :] < order[:, None])
-    spot = owner * CAP + jnp.sum(earlier.astype(jnp.int32), axis=1)
+    mode = lax.broadcasted_iota(jnp.int32, flat.shape, 0)
+    slot = lax.broadcasted_iota(jnp.int32, flat.shape, 1)
+    order = slot * 4 + mode
+    live = slot < live_count
+    earlier = (owner == owner[:, :, None, None]) & live & (order < order[:, :, None, None])
+    spot = owner * CAP + jnp.sum(earlier.astype(jnp.int32), axis=(2, 3))
     spot = jnp.where(live, spot, -1)
-    hit = spot[None, :] == jnp.arange(LANES)[:, None]
-    block = (order % 4) * local_blocks + flat - owner * local_blocks
-    want = jnp.max(jnp.where(hit, block[None, :], -1), axis=1)
-    inverse = jnp.max(jnp.where(hit, order[None, :], -1), axis=1)
+    hit = spot == jnp.arange(LANES)[:, None, None]
+    block = mode * local_blocks + flat - owner * local_blocks
+    want = jnp.max(jnp.where(hit, block, -1), axis=(1, 2))
+    inverse = jnp.max(jnp.where(hit, order, -1), axis=(1, 2))
     return jnp.maximum(spot, 0), want.reshape(1, LANES), inverse.reshape(1, LANES)
 
 

time: 73.8 us -> 70.6 us (0.957)
  Pallas kernels: 69.2 us -> 66.1 us
  local copies, waits for them, and re-layouts: 3.39 us -> 2.55 us
  other arithmetic: 0.31 us -> 1.1 us
    pallas_call x1, Pallas kernels: 69.2 us -> 66.1 us  [step(): pl.pallas_call(functools.partial(step_kernel, tiles, rows), out_shape=jax...]
    unnamed x4 -> x3, local copies, waits for them, and re-layouts: 3.31 us -> 2.55 us
    sub x1, other arithmetic: 0.02 us -> 0.76 us  [tables(): block = mode * local_blocks + flat - owner * local_blocks]
where the time goes in v4:
time: 70.6 us; the launch traced here: 70.5 us
  Pallas kernels  66.1 us (94%)
  local copies, waits for them, and re-layouts  2.55 us (4%)
  other arithmetic  1.1 us (2%)
    pallas_call x1, Pallas kernels, step(): pl.pallas_call(functools.partial(step_kernel, tiles, rows), out_shape=jax...  66.1 us
    unnamed x3, local copies, waits for them, and re-layouts  2.55 us

profile of v4, /device:TPU:0, one launch (start us, length us, event | category | flops | bytes accessed | tf_op | source)
XLA Modules:
  0.0 70.5 jit_solution(1894638289383524592)
XLA Ops:
  0.7 0.8 %bitcast_subtract_fusion = (s32[4,8]{1,0:T(4,128)S(1)}, s32[4,8]{1,0:T(4,128)S(1)}, s32[4,8]{1,0:T(4,128)S(1)}) fusion(s32[1,8,4]{1,2,0:T(4,128)} %param.5, s32[4]{0:T(128)S(1)} %iota_multiply_fusion, s32[8]{0:T(128)S(1)} %iota_multiply_fusion.1), kind=kLoop, calls=%fused_computation.5 | loop fusion | flops 384 | bytes 560 | tf_op jit(solution)/shard_map/sub | solution.py:331
  1.4 0.2 convert_reduce_fusion
  1.7 0.1 select_reduce_fusion
  1.8 0.0 copy-start
  1.8 1.4 %copy-done = f32[4,384,256]{2,1,0:T(8,128)S(1)} copy-done((f32[4,384,256]{2,1,0:T(8,128)S(1)}, f32[4,384,256]{2,1,0:T(8,128)}, u32[]{:S(2)}) %copy-start) | copy-done | bytes 1572888
  3.2 66.1 %gradient_step.1 = f32[48,32,256]{2,1,0:T(8,128)S(1)} custom-call(s32[4,8]{1,0:T(4,128)S(1)} %get-tuple-element.9.spot_ref, s32[1,128]{1,0:T(1,128)S(1)} %bitcast.37, s32[1,128]{1,0:T(1,128)S(1)} %bitcast.36, bf16[8,1024,1024]{2,1,0:T(8,128)(2,1)} %bitcast.39, f32[48,32,256]{2,1,0:T(8,128)S(1)} %bitcast.38), custom_call_target="tpu_custom_call" | custom-call | flops 12884901888 | bytes 16777216 | tf_op jit(solution)/shard_map/gradient_step/pallas_call | solution.py:293
  69.3 1.1 %copy.7 = f32[4,384,256]{2,1,0:T(8,128)} copy(f32[4,384,256]{2,1,0:T(8,128)S(1)} %bitcast.35) | data formatting | bytes 3145728
  (4 shorter events, 0.0 us)
Async XLA Ops:
  1.8 1.4 %copy-start = (f32[4,384,256]{2,1,0:T(8,128)S(1)}, f32[4,384,256]{2,1,0:T(8,128)}, u32[]{:S(2)}) copy-start(f32[4,384,256]{2,1,0:T(8,128)} %param.7) | copy-start | bytes 4718596

commit v5 on v4

--- a/solution.py
+++ b/solution.py
@@ -102,39 +102,52 @@
         index = spot_ref[mode, slot]
         return blocks[index // CAP, lax.rem(index, CAP)].astype(jnp.float32)
 
-    @pl.loop(0, slots)
-    def _(slot):
-        @pl.when(slot + 2 < slots)
-        def _():
-            tile_copy(slot + 2).start()
-
-        one, two, three, four = (block(slot, mode) for mode in range(4))
+    def work(slot, before):
+        if slot is not None:
+            now = slot % 2
+            one, two, three, four = (block(slot, mode) for mode in range(4))
+            for part in range(edge // group):
+                lines = slice(part * group, (part + 1) * group)
+                at = pl.ds(part * chunk, chunk)
+                pair_ab[now, at, :] = (one[lines][:, None, :] * two[None, :, :]).reshape(chunk, rank).astype(jnp.bfloat16)
+                pair_cd[at, :] = (three[lines][:, None, :] * four[None, :, :]).reshape(chunk, rank).astype(jnp.bfloat16)
+            tile_copy(slot).wait()
+            second = jnp.zeros((edge, rank), jnp.float32)
+        if before is not None:
+            past = before % 2
+            old_three, old_four = block(before, 2), block(before, 3)
+            fourth = jnp.zeros((edge, rank), jnp.float32)
         for part in range(edge // group):
             lines = slice(part * group, (part + 1) * group)
             at = pl.ds(part * chunk, chunk)
-            pair_ab[at, :] = (one[lines][:, None, :] * two[None, :, :]).reshape(chunk, rank).astype(jnp.bfloat16)
-            pair_cd[at, :] = (three[lines][:, None, :] * four[None, :, :]).reshape(chunk, rank).astype(jnp.bfloat16)
-        tile_copy(slot).wait()
-        second = jnp.zeros((edge, rank), jnp.float32)
-        for part in range(edge // group):
-            lines = slice(part * group, (part + 1) * group)
-            at = pl.ds(part * chunk, chunk)
-            model = lax.dot_general(pair_ab[at, :], pair_cd[...], (((1,), (1,)), ((), ())), preferred_element_type=jnp.float32)
-            off = jnp.clip(model - stack[slot, at, :].astype(jnp.float32), -1.0, 1.0).astype(jnp.bfloat16)
-            misfit[at, :] = off
-            left = jnp.dot(off, pair_cd[...], preferred_element_type=jnp.float32).reshape(group, edge, rank)
-            grads[slot * 4, lines, :] = jnp.sum(left * two[None, :, :], axis=1)
-            second = second + jnp.sum(left * one[lines][:, None, :], axis=0)
-        grads[slot * 4 + 1] = second
-        fourth = jnp.zeros((edge, rank), jnp.float32)
-        for part in range(edge // group):
-            lines = slice(part * group, (part + 1) * group)
-            at = pl.ds(part * chunk, chunk)
-            right = lax.dot_general(misfit[:, at], pair_ab[...], (((0,), (0,)), ((), ())), preferred_element_type=jnp.float32)
-            right = right.reshape(group, edge, rank)
-            grads[slot * 4 + 2, lines, :] = jnp.sum(right * four[None, :, :], axis=1)
-            fourth = fourth + jnp.sum(right * three[lines][:, None, :], axis=0)
-        grads[slot * 4 + 3] = fourth
+            if before is not None:
+                right = lax.dot_general(misfit[past, :, at], pair_ab[past], (((0,), (0,)), ((), ())), preferred_element_type=jnp.float32)
+                right = right.reshape(group, edge, rank)
+                grads[before * 4 + 2, lines, :] = jnp.sum(right * old_four[None, :, :], axis=1)
+                fourth = fourth + jnp.sum(right * old_three[lines][:, None, :], axis=0)
+            if slot is not None:
+                model = lax.dot_general(pair_ab[now, at, :], pair_cd[...], (((1,), (1,)), ((), ())), preferred_element_type=jnp.float32)
+                off = jnp.clip(model - stack[slot, at, :].astype(jnp.float32), -1.0, 1.0).astype(jnp.bfloat16)
+                misfit[now, at, :] = off
+                left = jnp.dot(off, pair_cd[...], preferred_element_type=jnp.float32).reshape(group, edge, rank)
+                grads[slot * 4, lines, :] = jnp.sum(left * two[None, :, :], axis=1)
+                second = second + jnp.sum(left * one[lines][:, None, :], axis=0)
+        if slot is not None:
+            grads[slot * 4 + 1] = second
+        if before is not None:
+            grads[before * 4 + 3] = fourth
+
+    work(0, None)
+
+    @pl.loop(1, slots)
+    def _(slot):
+        @pl.when(slot + 1 < slots)
+        def _():
+            tile_copy(slot + 1).start()
+
+        work(slot, slot - 1)
+
+    work(None, slots - 1)
 
     share = TILE // tiles
     span = CAP * share
@@ -302,7 +315,7 @@
             pltpu.SMEM((rows, 1, LANES), jnp.int32),
             bf16(rows, CAP, TILE, rank),
             bf16(rows, CAP, TILE, rank),
-            bf16(height, rank), bf16(width, rank), bf16(height, width),
+            bf16(2, height, rank), bf16(width, rank), bf16(2, height, width),
             pltpu.VMEM((slots * 4, TILE, rank), jnp.float32),
             bf16(peers, span, rank),
             bf16(peers, span, rank),

time: 70.6 us -> 73.5 us (1.041)
  Pallas kernels: 66.1 us -> 69 us
    pallas_call x1, Pallas kernels: 66.1 us -> 69 us  [step(): pl.pallas_call(functools.partial(step_kernel, tiles, rows), out_shape=jax...]
where the time goes in v5:
time: 73.5 us; the launch traced here: 73.3 us
  Pallas kernels  69 us (94%)
  local copies, waits for them, and re-layouts  2.55 us (3%)
  other arithmetic  1.1 us (1%)
    pallas_call x1, Pallas kernels, step(): pl.pallas_call(functools.partial(step_kernel, tiles, rows), out_shape=jax...  69 us
    unnamed x3, local copies, waits for them, and re-layouts  2.55 us

profile of v5, /device:TPU:0, one launch (start us, length us, event | category | flops | bytes accessed | tf_op | source)
XLA Modules:
  0.0 73.3 jit_solution(3740920603546802554)
XLA Ops:
  0.7 0.8 %bitcast_subtract_fusion = (s32[4,8]{1,0:T(4,128)S(1)}, s32[4,8]{1,0:T(4,128)S(1)}, s32[4,8]{1,0:T(4,128)S(1)}) fusion(s32[1,8,4]{1,2,0:T(4,128)} %param.5, s32[4]{0:T(128)S(1)} %iota_multiply_fusion, s32[8]{0:T(128)S(1)} %iota_multiply_fusion.1), kind=kLoop, calls=%fused_computation.5 | loop fusion | flops 384 | bytes 560 | tf_op jit(solution)/shard_map/sub | solution.py:344
  1.4 0.2 convert_reduce_fusion
  1.7 0.1 select_reduce_fusion
  1.8 0.0 copy-start
  1.8 1.4 %copy-done = f32[4,384,256]{2,1,0:T(8,128)S(1)} copy-done((f32[4,384,256]{2,1,0:T(8,128)S(1)}, f32[4,384,256]{2,1,0:T(8,128)}, u32[]{:S(2)}) %copy-start) | copy-done | bytes 1572888
  3.2 69.0 %gradient_step.1 = f32[48,32,256]{2,1,0:T(8,128)S(1)} custom-call(s32[4,8]{1,0:T(4,128)S(1)} %get-tuple-element.9.spot_ref, s32[1,128]{1,0:T(1,128)S(1)} %bitcast.37, s32[1,128]{1,0:T(1,128)S(1)} %bitcast.36, bf16[8,1024,1024]{2,1,0:T(8,128)(2,1)} %bitcast.39, f32[48,32,256]{2,1,0:T(8,128)S(1)} %bitcast.38), custom_call_target="tpu_custom_call" | custom-call | flops 12884901888 | bytes 16777216 | tf_op jit(solution)/shard_map/gradient_step/pallas_call | solution.py:306
  72.2 1.1 %copy.7 = f32[4,384,256]{2,1,0:T(8,128)} copy(f32[4,384,256]{2,1,0:T(8,128)S(1)} %bitcast.35) | data formatting | bytes 3145728
  (4 shorter events, 0.0 us)
Async XLA Ops:
  1.8 1.4 %copy-start = (f32[4,384,256]{2,1,0:T(8,128)S(1)}, f32[4,384,256]{2,1,0:T(8,128)}, u32[]{:S(2)}) copy-start(f32[4,384,256]{2,1,0:T(8,128)} %param.7) | copy-start | bytes 4718596

commit v6 on v4

--- a/solution.py
+++ b/solution.py
@@ -96,7 +96,7 @@
         block_copy(peer, peer).wait_recv()
 
     edge = TILE
-    chunk = 256
+    chunk = 512
     group = chunk // edge
     def block(slot, mode):
         index = spot_ref[mode, slot]

time: 70.6 us -> 70.6 us (level)
  no operation moved by 1% of the time
where the time goes in v6:
time: 70.6 us; the launch traced here: 70.5 us
  Pallas kernels  66.1 us (94%)
  local copies, waits for them, and re-layouts  2.55 us (4%)
  other arithmetic  1.1 us (2%)
    pallas_call x1, Pallas kernels, step(): pl.pallas_call(functools.partial(step_kernel, tiles, rows), out_shape=jax...  66.1 us
    unnamed x3, local copies, waits for them, and re-layouts  2.55 us

profile of v6, /device:TPU:0, one launch (start us, length us, event | category | flops | bytes accessed | tf_op | source)
XLA Modules:
  0.0 70.5 jit_solution(18119341596976442041)
XLA Ops:
  0.7 0.8 %bitcast_subtract_fusion = (s32[4,8]{1,0:T(4,128)S(1)}, s32[4,8]{1,0:T(4,128)S(1)}, s32[4,8]{1,0:T(4,128)S(1)}) fusion(s32[1,8,4]{1,2,0:T(4,128)} %param.5, s32[4]{0:T(128)S(1)} %iota_multiply_fusion, s32[8]{0:T(128)S(1)} %iota_multiply_fusion.1), kind=kLoop, calls=%fused_computation.5 | loop fusion | flops 384 | bytes 560 | tf_op jit(solution)/shard_map/sub | solution.py:331
  1.4 0.2 convert_reduce_fusion
  1.7 0.1 select_reduce_fusion
  1.8 0.0 copy-start
  1.8 1.4 %copy-done = f32[4,384,256]{2,1,0:T(8,128)S(1)} copy-done((f32[4,384,256]{2,1,0:T(8,128)S(1)}, f32[4,384,256]{2,1,0:T(8,128)}, u32[]{:S(2)}) %copy-start) | copy-done | bytes 1572888
  3.2 66.1 %gradient_step.1 = f32[48,32,256]{2,1,0:T(8,128)S(1)} custom-call(s32[4,8]{1,0:T(4,128)S(1)} %get-tuple-element.9.spot_ref, s32[1,128]{1,0:T(1,128)S(1)} %bitcast.37, s32[1,128]{1,0:T(1,128)S(1)} %bitcast.36, bf16[8,1024,1024]{2,1,0:T(8,128)(2,1)} %bitcast.39, f32[48,32,256]{2,1,0:T(8,128)S(1)} %bitcast.38), custom_call_target="tpu_custom_call" | custom-call | flops 12884901888 | bytes 16777216 | tf_op jit(solution)/shard_map/gradient_step/pallas_call | solution.py:293
  69.3 1.1 %copy.7 = f32[4,384,256]{2,1,0:T(8,128)} copy(f32[4,384,256]{2,1,0:T(8,128)S(1)} %bitcast.35) | data formatting | bytes 3145728
  (4 shorter events, 0.0 us)
Async XLA Ops:
  1.8 1.4 %copy-start = (f32[4,384,256]{2,1,0:T(8,128)S(1)}, f32[4,384,256]{2,1,0:T(8,128)}, u32[]{:S(2)}) copy-start(f32[4,384,256]{2,1,0:T(8,128)} %param.7) | copy-start | bytes 4718596
